TPU v7x, 32 devices: a whole 2x2x4 slice. The times are simulated.
32 devices in a mesh: blk: 8 (over z, y), grp: 4 (over x, core).
Axes of the slice: x: 2, y: 2, z: 4, core: 2. Of those that a mesh axis runs over, the one named last changes fastest.
Arguments:
- images: bfloat16 [2048, 1536], P('blk'), may hold values from -100 to 100
- defocus: float32 [2048], P('blk'), may hold values from 1 to 12
- class_id: int32 [2048, 1], P('blk'), may hold values from 0 to 63; in each aligned block of 256 rows (0 to 255, 256 to 511, ...) at most 10 rows name the same one
- rotation_id: int32 [2048], P('blk'), may hold values from 0 to 31
- shift_id: int32 [2048], P('blk'), may hold values from 0 to 8
- references: float32 [4, 16, 1536], P('grp', 'blk'), may hold values from -4 to 4
- owner: int32 [4, 16], P('grp'), may hold values from 0 to 15, as said below
- inv_noise: float32 [24], replicated, may hold values from 0.5 to 2
- prior: float32 [24], replicated, may hold values from 0.5 to 2
Outputs:
- evidence: float32 [2048], P('blk')
- new_refs: float32 [4, 16, 1536], P('grp', 'blk')
Inputs may be any that keep to these rules, and one draw needn't show every extreme that they name: `class_id`: among the particles of one index of blk, no class is assigned to more than 10 particles, and some class to exactly 10. `owner`: each row is a permutation of 0 to 15.
All inputs are finite; a program needn't handle non-finite values.
Results may differ from a plain program's by a relative error of at most 0.0036.
Values sent between devices are 32-bit elements; how exact they have to be, the bound alone decides.
A program may use at most 64 MiB of HBM per device.

v0:
```python
import math

import jax
import jax.numpy as jnp
from jax import lax
from jax.sharding import PartitionSpec as P

CYCLES = 24
ANGLES = 32
SHIFTS = 9
CL_DEV = 2


def contrast_table(defocus):
    frequency = (jnp.arange(CYCLES, dtype=jnp.float32) + 1.0) / CYCLES
    return -jnp.sin(defocus[:, None] * (frequency * frequency)[None, :] + 0.15)


def phase_tables():
    radius = (jnp.arange(CYCLES, dtype=jnp.float32) + 1.0) / (2.0 * CYCLES)
    bearing = 2.0 * math.pi / ANGLES * jnp.arange(ANGLES, dtype=jnp.float32)
    shift_index = jnp.arange(SHIFTS, dtype=jnp.int32)
    shift_x = (shift_index // 3 - 1).astype(jnp.float32)
    shift_y = (shift_index % 3 - 1).astype(jnp.float32)
    along = (
        shift_x[:, None] * jnp.cos(bearing)[None, :] + shift_y[:, None] * jnp.sin(bearing)[None, :]
    )
    phase = -2.0 * math.pi * radius[None, :, None] * along[:, None, :]
    return (jnp.cos(phase), jnp.sin(phase))


def weigh(images, factor):
    row_total = images.shape[0]
    grid = images.astype(jnp.float32).reshape(row_total, 2, CYCLES, ANGLES)
    return (grid * factor[:, None, :, None]).reshape(row_total, -1).astype(jnp.bfloat16)


def make_templates(ref_block):
    block_rows = ref_block.shape[0]
    grid = ref_block.reshape(block_rows, 2, CYCLES, ANGLES)
    angular = jnp.arange(ANGLES, dtype=jnp.int32)
    turning = (
        angular[:, None, None] == (angular[None, None, :] - angular[None, :, None]) % ANGLES
    ).astype(jnp.float32)
    rotated = jnp.einsum("nqka,arb->nrqkb", grid, turning, precision=lax.Precision.HIGHEST)
    phase_cos, phase_sin = phase_tables()
    rotated_re = rotated[:, :, 0][:, :, None]
    rotated_im = rotated[:, :, 1][:, :, None]
    real_part = phase_cos[None, None] * rotated_re - phase_sin[None, None] * rotated_im
    imag_part = phase_sin[None, None] * rotated_re + phase_cos[None, None] * rotated_im
    stacked = jnp.stack([real_part, imag_part], axis=3)
    return stacked.reshape(block_rows * ANGLES * SHIFTS, -1).astype(jnp.bfloat16)


def score_block(ref_block, weighted, contrast_power, score_scale):
    block_rows = ref_block.shape[0]
    templates = make_templates(ref_block)
    cross = lax.dot_general(
        templates, weighted, (((1,), (1,)), ((), ())), preferred_element_type=jnp.float32
    )
    grid = ref_block.reshape(block_rows, 2, CYCLES, ANGLES)
    power = jnp.sum(grid * grid, axis=(1, 3))
    penalty = jnp.dot(power, contrast_power.T, precision=lax.Precision.HIGHEST)
    logits = (
        cross.reshape(block_rows, ANGLES * SHIFTS, -1) - 0.5 * penalty[:, None, :]
    ) * score_scale
    return logits.reshape(block_rows * ANGLES * SHIFTS, -1)


def target_rows(relative, rotation_id, shift_id):
    inside = (relative >= 0) & (relative < CL_DEV)
    return jnp.where(inside, (relative * ANGLES + rotation_id) * SHIFTS + shift_id, -1)


def update(running, logits, target):
    peak, total, picked = running
    new_peak = jnp.maximum(peak, jnp.max(logits, axis=0))
    total = total * jnp.exp(peak - new_peak) + jnp.sum(jnp.exp(logits - new_peak[None, :]), axis=0)
    row_index = jnp.arange(logits.shape[0], dtype=jnp.int32)
    picked = picked + jnp.sum(jnp.where(row_index[:, None] == target[None, :], logits, 0.0), axis=0)
    return (new_peak, total, picked)


def align_terms(images, contrast, weight, rotation_id, shift_id):
    row_total = images.shape[0]
    phase_cos, phase_sin = phase_tables()
    chosen = (shift_id[:, None] == jnp.arange(SHIFTS, dtype=jnp.int32)[None, :]).astype(jnp.float32)
    cos_rows = jnp.dot(
        chosen, phase_cos.reshape(SHIFTS, -1), precision=lax.Precision.HIGHEST
    ).reshape(row_total, CYCLES, ANGLES)
    sin_rows = jnp.dot(
        chosen, phase_sin.reshape(SHIFTS, -1), precision=lax.Precision.HIGHEST
    ).reshape(row_total, CYCLES, ANGLES)
    grid = images.astype(jnp.float32).reshape(row_total, 2, CYCLES, ANGLES)
    unshift_re = cos_rows * grid[:, 0] + sin_rows * grid[:, 1]
    unshift_im = cos_rows * grid[:, 1] - sin_rows * grid[:, 0]
    unshifted = jnp.stack([unshift_re, unshift_im], axis=1)
    angular = jnp.arange(ANGLES, dtype=jnp.int32)
    turning = (
        angular[None, :, None] == (angular[None, None, :] + rotation_id[:, None, None]) % ANGLES
    ).astype(jnp.float32)
    aligned = jnp.einsum("pqka,pab->pqkb", unshifted, turning, precision=lax.Precision.HIGHEST)
    scaled = weight[:, None] * contrast
    numer_term = (aligned * scaled[:, None, :, None]).reshape(row_total, -1)
    denom_term = weight[:, None] * contrast * contrast
    return (numer_term, denom_term)


def finish(numerator, denominator, prior):
    grid = numerator.reshape(-1, 2, CYCLES, ANGLES)
    return (grid / (denominator + prior[None, :])[:, None, :, None]).reshape(numerator.shape)


def shards(images, defocus, class_id, rotation_id, shift_id, references, owner, inv_noise, prior):
    particle_count = images.shape[0]
    group_classes = owner.shape[1]
    class_total = group_classes * lax.axis_size("grp")
    contrast = contrast_table(defocus)
    contrast_power = contrast * contrast * inv_noise[None, :]
    weighted = weigh(images, contrast * inv_noise[None, :])
    score_scale = 1.0 / math.sqrt(images.shape[1])
    local_class = class_id[:, 0] - lax.axis_index("grp") * group_classes
    member = (local_class >= 0) & (local_class < group_classes)
    initial = (
        jnp.full((particle_count,), -1e30, jnp.float32),
        jnp.zeros((particle_count,), jnp.float32),
        jnp.zeros((particle_count,), jnp.float32),
    )
    running = initial
    shard_piece = lax.all_gather(references, "blk", axis=1, tiled=True)
    blocks = shard_piece[0].reshape(-1, CL_DEV, shard_piece.shape[2])
    firsts = CL_DEV * jnp.arange(blocks.shape[0], dtype=jnp.int32)

    def advance(running_state, entries):
        ref_block, block_first = entries
        logits = score_block(ref_block, weighted, contrast_power, score_scale)
        return (
            update(
                running_state, logits, target_rows(local_class - block_first, rotation_id, shift_id)
            ),
            None,
        )

    running, unused = lax.scan(advance, running, (blocks, firsts))
    peak, total, picked = running
    global_peak = lax.pmax(peak, "grp")
    global_total = lax.psum(total * jnp.exp(peak - global_peak), "grp")
    log_sum = global_peak + jnp.log(global_total)
    log_orients = math.log(class_total * ANGLES * SHIFTS)
    evidence = log_sum - log_orients
    weight = jnp.where(member, jnp.exp(jnp.where(member, picked - log_sum + log_orients, 0.0)), 0.0)
    numer_term, denom_term = align_terms(images, contrast, weight, rotation_id, shift_id)
    safe_class = jnp.where(member, local_class, 0)
    class_index = jnp.arange(group_classes, dtype=jnp.int32)
    slot = jnp.sum(
        jnp.where(safe_class[:, None] == class_index[None, :], owner[0][None, :], 0), axis=1
    )
    owning = (class_index[:, None] == jnp.where(member, slot, -1)[None, :]).astype(jnp.float32)
    partial_numer = jnp.dot(owning, numer_term, precision=lax.Precision.HIGHEST)
    partial_denom = jnp.dot(owning, denom_term, precision=lax.Precision.HIGHEST)
    numerator, denominator = (
        lax.psum_scatter(partial_numer, "blk", scatter_dimension=0, tiled=True),
        lax.psum_scatter(partial_denom, "blk", scatter_dimension=0, tiled=True),
    )
    new_refs = finish(numerator, denominator, prior)[None]
    return (evidence, new_refs)


def solution(mesh):
    in_specs = (
        P("blk", None),
        P("blk"),
        P("blk", None),
        P("blk"),
        P("blk"),
        P("grp", "blk", None),
        P("grp", None),
        P(),
        P(),
    )
    out_specs = (P("blk"), P("grp", "blk", None))
    return jax.shard_map(shards, mesh=mesh, in_specs=in_specs, out_specs=out_specs, check_vma=False)
```

profile of v0, /device:TPU:0, one launch (start us, length us, event | category | flops | bytes accessed | tf_op | source)
XLA Modules:
  0.0 327.8 jit_solution(3096894273756106286)
XLA Ops:
  7.9 0.7 copy.46
  8.6 32.3 %all_gather.3 = f32[1,16,1536]{2,0,1:T(1,128)S(1)} all-gather(f32[1,2,1536]{2,0,1:T(1,128)S(1)} %copy.46), channel_id=1, replica_groups=mesh['blk'=8,'grp'=4] {'blk'}, dimensions={1}, use_global_device_ids=true | all-gather | bytes 110592 | tf_op jit(solution)/shard_map/all_gather | solution.py:130
  41.3 1.4 copy.47
  42.7 0.9 fusion.47
  43.7 1.1 copy.48
  45.0 167.6 %while.18 = (s32[]{:T(128)}, f32[256]{0:T(256)S(1)}, f32[256]{0:T(256)S(1)}, f32[256]{0:T(256)S(1)}, f32[8,2,1536]{2,1,0:T(2,128)S(1)}, /*index=5*/bf16[256,1536...) while((s32[]{:T(128)}, f32[256]{0:T(256)S(1)}, ...), condition=%wide.region_5.6_spmd.clone, body=%wide.region_0.5_spmd.clone.sunk | while | flops 496573632 | bytes 14409028 | solution.py:144
  46.3 0.8 convolution_bitcast_fusion.2
  47.2 2.1 subtract_convert_fusion.2
  49.3 4.4 %pad_maximum_fusion.3 = bf16[2,32,9,2,24,32]{5,4,3,2,1,0:T(8,128)(2,1)} fusion(bf16[2,32,9,1,24,32]{5,4,3,2,1,0:T(8,128)(2,1)S(1)} %get-tuple-element.435, bf16[2,32,9,1,24,32]{5,4,3,2,1,0:T(8,128)(2,1)S(1)} %get-tuple-element.436), kind=kLoop, calls=%fused_computation.1.clone.1 | loop fusion | flops 884736 | bytes 3538944 | tf_op jit(solution)/shard_map/while/body/eval_jaxpr/stack | solution.py:51
  53.7 8.9 %convert_element_type.90 = bf16[2,288,1536]{2,1,0:T(8,128)(2,1)S(1)} reshape(bf16[2,32,9,2,24,32]{5,4,3,2,1,0:T(8,128)(2,1)} %pad_maximum_fusion.3) | data formatting | bytes 3538944 | tf_op jit(solution)/shard_map/while/body/eval_jaxpr/convert_element_type | solution.py:52
  62.6 1.8 fusion.105
  65.1 0.7 and_select_fusion.7
  67.3 0.8 convolution_bitcast_fusion.2
  68.2 2.1 subtract_convert_fusion.2
  70.2 4.4 %pad_maximum_fusion.3 = bf16[2,32,9,2,24,32]{5,4,3,2,1,0:T(8,128)(2,1)} fusion(bf16[2,32,9,1,24,32]{5,4,3,2,1,0:T(8,128)(2,1)S(1)} %get-tuple-element.435, bf16[2,32,9,1,24,32]{5,4,3,2,1,0:T(8,128)(2,1)S(1)} %get-tuple-element.436), kind=kLoop, calls=%fused_computation.1.clone.1 | loop fusion | flops 884736 | bytes 3538944 | tf_op jit(solution)/shard_map/while/body/eval_jaxpr/stack | solution.py:51
  74.6 8.9 %convert_element_type.90 = bf16[2,288,1536]{2,1,0:T(8,128)(2,1)S(1)} reshape(bf16[2,32,9,2,24,32]{5,4,3,2,1,0:T(8,128)(2,1)} %pad_maximum_fusion.3) | data formatting | bytes 3538944 | tf_op jit(solution)/shard_map/while/body/eval_jaxpr/convert_element_type | solution.py:52
  83.5 1.8 fusion.105
  86.0 0.7 and_select_fusion.7
  88.2 0.8 convolution_bitcast_fusion.2
  89.1 2.1 subtract_convert_fusion.2
  91.2 4.4 %pad_maximum_fusion.3 = bf16[2,32,9,2,24,32]{5,4,3,2,1,0:T(8,128)(2,1)} fusion(bf16[2,32,9,1,24,32]{5,4,3,2,1,0:T(8,128)(2,1)S(1)} %get-tuple-element.435, bf16[2,32,9,1,24,32]{5,4,3,2,1,0:T(8,128)(2,1)S(1)} %get-tuple-element.436), kind=kLoop, calls=%fused_computation.1.clone.1 | loop fusion | flops 884736 | bytes 3538944 | tf_op jit(solution)/shard_map/while/body/eval_jaxpr/stack | solution.py:51
  95.6 8.9 %convert_element_type.90 = bf16[2,288,1536]{2,1,0:T(8,128)(2,1)S(1)} reshape(bf16[2,32,9,2,24,32]{5,4,3,2,1,0:T(8,128)(2,1)} %pad_maximum_fusion.3) | data formatting | bytes 3538944 | tf_op jit(solution)/shard_map/while/body/eval_jaxpr/convert_element_type | solution.py:52
  104.5 1.8 fusion.105
  107.0 0.7 and_select_fusion.7
  109.2 0.8 convolution_bitcast_fusion.2
  110.1 2.1 subtract_convert_fusion.2
  112.1 4.4 %pad_maximum_fusion.3 = bf16[2,32,9,2,24,32]{5,4,3,2,1,0:T(8,128)(2,1)} fusion(bf16[2,32,9,1,24,32]{5,4,3,2,1,0:T(8,128)(2,1)S(1)} %get-tuple-element.435, bf16[2,32,9,1,24,32]{5,4,3,2,1,0:T(8,128)(2,1)S(1)} %get-tuple-element.436), kind=kLoop, calls=%fused_computation.1.clone.1 | loop fusion | flops 884736 | bytes 3538944 | tf_op jit(solution)/shard_map/while/body/eval_jaxpr/stack | solution.py:51
  116.5 8.9 %convert_element_type.90 = bf16[2,288,1536]{2,1,0:T(8,128)(2,1)S(1)} reshape(bf16[2,32,9,2,24,32]{5,4,3,2,1,0:T(8,128)(2,1)} %pad_maximum_fusion.3) | data formatting | bytes 3538944 | tf_op jit(solution)/shard_map/while/body/eval_jaxpr/convert_element_type | solution.py:52
  125.4 1.8 fusion.105
  127.9 0.7 and_select_fusion.7
  130.1 0.8 convolution_bitcast_fusion.2
  131.0 2.1 subtract_convert_fusion.2
  133.1 4.4 %pad_maximum_fusion.3 = bf16[2,32,9,2,24,32]{5,4,3,2,1,0:T(8,128)(2,1)} fusion(bf16[2,32,9,1,24,32]{5,4,3,2,1,0:T(8,128)(2,1)S(1)} %get-tuple-element.435, bf16[2,32,9,1,24,32]{5,4,3,2,1,0:T(8,128)(2,1)S(1)} %get-tuple-element.436), kind=kLoop, calls=%fused_computation.1.clone.1 | loop fusion | flops 884736 | bytes 3538944 | tf_op jit(solution)/shard_map/while/body/eval_jaxpr/stack | solution.py:51
  137.4 8.9 %convert_element_type.90 = bf16[2,288,1536]{2,1,0:T(8,128)(2,1)S(1)} reshape(bf16[2,32,9,2,24,32]{5,4,3,2,1,0:T(8,128)(2,1)} %pad_maximum_fusion.3) | data formatting | bytes 3538944 | tf_op jit(solution)/shard_map/while/body/eval_jaxpr/convert_element_type | solution.py:52
  146.4 1.8 fusion.105
  148.8 0.7 and_select_fusion.7
  151.1 0.8 convolution_bitcast_fusion.2
  152.0 2.1 subtract_convert_fusion.2
  154.0 4.4 %pad_maximum_fusion.3 = bf16[2,32,9,2,24,32]{5,4,3,2,1,0:T(8,128)(2,1)} fusion(bf16[2,32,9,1,24,32]{5,4,3,2,1,0:T(8,128)(2,1)S(1)} %get-tuple-element.435, bf16[2,32,9,1,24,32]{5,4,3,2,1,0:T(8,128)(2,1)S(1)} %get-tuple-element.436), kind=kLoop, calls=%fused_computation.1.clone.1 | loop fusion | flops 884736 | bytes 3538944 | tf_op jit(solution)/shard_map/while/body/eval_jaxpr/stack | solution.py:51
  158.4 8.9 %convert_element_type.90 = bf16[2,288,1536]{2,1,0:T(8,128)(2,1)S(1)} reshape(bf16[2,32,9,2,24,32]{5,4,3,2,1,0:T(8,128)(2,1)} %pad_maximum_fusion.3) | data formatting | bytes 3538944 | tf_op jit(solution)/shard_map/while/body/eval_jaxpr/convert_element_type | solution.py:52
  167.3 1.8 fusion.105
  172.0 0.8 convolution_bitcast_fusion.2
  172.9 2.1 subtract_convert_fusion.2
  175.0 4.4 %pad_maximum_fusion.3 = bf16[2,32,9,2,24,32]{5,4,3,2,1,0:T(8,128)(2,1)} fusion(bf16[2,32,9,1,24,32]{5,4,3,2,1,0:T(8,128)(2,1)S(1)} %get-tuple-element.435, bf16[2,32,9,1,24,32]{5,4,3,2,1,0:T(8,128)(2,1)S(1)} %get-tuple-element.436), kind=kLoop, calls=%fused_computation.1.clone.1 | loop fusion | flops 884736 | bytes 3538944 | tf_op jit(solution)/shard_map/while/body/eval_jaxpr/stack | solution.py:51
  179.3 8.9 %convert_element_type.90 = bf16[2,288,1536]{2,1,0:T(8,128)(2,1)S(1)} reshape(bf16[2,32,9,2,24,32]{5,4,3,2,1,0:T(8,128)(2,1)} %pad_maximum_fusion.3) | data formatting | bytes 3538944 | tf_op jit(solution)/shard_map/while/body/eval_jaxpr/convert_element_type | solution.py:52
  188.3 1.8 fusion.105
  193.0 0.8 convolution_bitcast_fusion.2
  193.9 2.1 subtract_convert_fusion.2
  195.9 4.4 %pad_maximum_fusion.3 = bf16[2,32,9,2,24,32]{5,4,3,2,1,0:T(8,128)(2,1)} fusion(bf16[2,32,9,1,24,32]{5,4,3,2,1,0:T(8,128)(2,1)S(1)} %get-tuple-element.435, bf16[2,32,9,1,24,32]{5,4,3,2,1,0:T(8,128)(2,1)S(1)} %get-tuple-element.436), kind=kLoop, calls=%fused_computation.1.clone.1 | loop fusion | flops 884736 | bytes 3538944 | tf_op jit(solution)/shard_map/while/body/eval_jaxpr/stack | solution.py:51
  200.3 8.9 %convert_element_type.90 = bf16[2,288,1536]{2,1,0:T(8,128)(2,1)S(1)} reshape(bf16[2,32,9,2,24,32]{5,4,3,2,1,0:T(8,128)(2,1)} %pad_maximum_fusion.3) | data formatting | bytes 3538944 | tf_op jit(solution)/shard_map/while/body/eval_jaxpr/convert_element_type | solution.py:52
  209.2 1.8 fusion.105
  211.7 0.7 and_select_fusion.7
  212.6 5.7 %pmax.7 = f32[256]{0:T(256)S(1)} all-reduce(f32[256]{0:T(256)S(1)} %get-tuple-element.188), channel_id=1, replica_groups=mesh['blk'=8,'grp'=4] {'grp'}, use_global_device_ids=true, to_apply=%region_6.7 | all-reduce | flops 256 | bytes 2048 | tf_op jit(solution)/shard_map/pmax | solution.py:146
  218.3 6.8 %psum.7 = f32[256]{0:T(256)S(1)} all-reduce(f32[256]{0:T(256)S(1)} %exponential_multiply_fusion), channel_id=1, replica_groups=mesh['blk'=8,'grp'=4] {'grp'}, use_global_device_ids=true, to_apply=%region_7.8 | all-reduce | flops 256 | bytes 2048 | tf_op jit(solution)/shard_map/psum | solution.py:147
  226.0 0.7 multiply_add_fusion.2
  227.0 0.8 cosine_bitcast_fusion
  228.7 0.9 dot_general.41
  230.3 5.2 %copy.51 = f32[256,2,24,32]{3,2,1,0:T(8,128)} copy(f32[256,2,24,32]{0,3,2,1:T(8,128)S(1)} %pad_maximum_fusion.1) | data formatting | bytes 3145728 | tf_op jit(solution)/shard_map/stack | solution.py:97
  235.5 7.6 %broadcast_multiply_fusion = f32[256,2,24,32]{3,2,1,0:T(8,128)} fusion(f32[256,24]{1,0:T(8,128)S(1)} %copy.52, f32[256,2,24,32]{3,2,1,0:T(8,128)} %copy.51, s32[256,32]{1,0:T(8,128)S(1)} %add_select_fusion.1), kind=kOutput, calls=%fused_computation.61 | convolution fusion | flops 151650304 | bytes 3203072 | tf_op jit(solution)/shard_map/pqka,pab->pqkb/dot_general | solution.py:102
  243.1 5.1 %copy.53 = f32[256,2,24,32]{0,3,2,1:T(8,128)S(1)} copy(f32[256,2,24,32]{3,2,1,0:T(8,128)} %broadcast_multiply_fusion) | data formatting | bytes 3145728 | tf_op jit(solution)/shard_map/mul | solution.py:104
  248.2 1.5 fusion.48
  249.9 21.7 %all-reduce.1 = f32[16,24]{1,0:T(8,128)S(1)} all-reduce(f32[16,24]{1,0:T(8,128)S(1)} %fusion.44), channel_id=3, replica_groups=mesh['blk'=8,'grp'=4] {'blk'}, use_global_device_ids=true, to_apply=%region_10.11.clone | all-reduce | flops 384 | bytes 3072
  273.0 46.5 %all-reduce.4.cloned.1.call-done = f32[16,1536]{1,0:T(8,128)} async-done(((f32[16,1536]{1,0:T(8,128)}), f32[16,1536]{1,0:T(8,128)}) %all-reduce.4.cloned.1.call-update) | async-done | bytes 98320
  319.5 1.4 fusion.55
  (213 shorter events, 24.3 us)
Async XLA Ops:
  7.2 37.8 %copy-start.6 = (f32[24]{0:T(128)S(1)}, f32[24]{0:T(128)}, u32[]{:S(2)}) copy-start(f32[24]{0:T(128)} %param.18) | copy-start | bytes 292
  7.2 37.8 %copy-start.2 = (f32[256]{0:T(256)S(1)}, f32[256]{0:T(256)}, u32[]{:S(2)}) copy-start(f32[256]{0:T(256)} %param.12) | copy-start | bytes 3076
  7.2 37.6 %copy-start.1 = (s32[256]{0:T(256)S(1)}, s32[256]{0:T(256)}, u32[]{:S(2)}) copy-start(s32[256]{0:T(256)} %param.14) | copy-start | bytes 3076
  7.2 37.8 %copy-start.3 = (s32[256,1]{0,1:T(1,128)S(1)}, s32[256,1]{0,1:T(1,128)}, u32[]{:S(2)}) copy-start(s32[256,1]{0,1:T(1,128)} %param.13) | copy-start | bytes 3076
  7.2 37.8 %copy-start = (s32[256]{0:T(256)S(1)}, s32[256]{0:T(256)}, u32[]{:S(2)}) copy-start(s32[256]{0:T(256)} %param.15) | copy-start | bytes 3076
  7.2 312.3 %all-reduce.4.cloned.1.call-start = ((), (), s32[]{:S(2)}) async-start(), calls=%async_computation | async-start | bytes 196608
  45.0 180.1 %copy-start.4 = (s32[1,16]{1,0:T(1,128)S(1)}, s32[1,16]{1,0:T(1,128)}, u32[]{:S(2)}) copy-start(s32[1,16]{1,0:T(1,128)} %param.17) | copy-start | bytes 196
  243.1 28.5 %copy-start.7 = (u32[32]{0:T(128)S(1)}, u32[32]{0:T(128)}, u32[]{:S(2)}) copy-start(u32[32]{0:T(128)} %constant.209) | copy-start | bytes 388
  243.1 29.8 %copy-start.5 = (f32[24]{0:T(128)S(1)}, f32[24]{0:T(128)}, u32[]{:S(2)}) copy-start(f32[24]{0:T(128)} %param.19) | copy-start | bytes 292
Sparse Core Ops, SparseCore 0:
  249.8 69.7 all-reduce.3
where the time goes:
time: 330 us; the launch traced here: 328 us
  local copies, waits for them, and re-layouts  94.8 us (29%)
  other arithmetic  70.8 us (21%)
  blocking collectives  66.4 us (20%)
  waiting for transfers between devices  46.5 us (14%)
  matrix products  33.3 us (10%)
  between operations  15 us (5%)
    convert_element_type x8, local copies, waits for them, and re-layouts, make_templates(): stacked.reshape(block_rows * ANGLES * SHIFTS, -1).astype(jnp.bfloat16)  71.3 us
    unnamed x2, waiting for transfers between devices  46.5 us
    another operation x8, other arithmetic, make_templates(): stacked = jnp.stack([real_part, imag_part], axis=3)  34.9 us
    all_gather x1, blocking collectives, shards(): shard_piece = lax.all_gather(references, 'blk', axis=1, tiled=True)  32.3 us
    unnamed x1, blocking collectives  21.7 us
    another operation x8, other arithmetic  16.4 us
    dot_general x8, matrix products, score_block(): lax.dot_general(templates, weighted, (((1,), (1,)), ((), ())), preferred_...  14.4 us
    dot_general x1, matrix products, align_terms(): jnp.einsum('pqka,pab->pqkb', unshifted, turning, precision=lax.Precision....  7.58 us
  transfers between devices with their start and end apart: 1, of which 1 were waited for; matrix products, arithmetic and copies ran while one was open for 0% of the time, Pallas kernels for 0%

commit v1 on v0

v1 whole, which is shorter than its diff:
```python
import functools
import math

import jax
import jax.numpy as jnp
import numpy as np
from jax import lax
from jax.experimental import pallas as pl
from jax.experimental.pallas import tpu as pltpu
from jax.sharding import PartitionSpec as P

CYCLES = 24
ANGLES = 32
SHIFTS = 9
HALF = CYCLES * ANGLES
FEAT = 2 * HALF
LANES = 128
CHUNKS = FEAT // LANES
FOLDED = HALF // 2
FOLDS = FOLDED // LANES
BEND = ANGLES // 2
PAIRS = ((0, 8), (1, 7), (2, 6), (3, 5))
MESH = pl.DeviceIdType.MESH
F32 = jnp.float32
BF16 = jnp.bfloat16
NT = (((1,), (1,)), ((), ()))


def phase_numpy():
    radius = (np.arange(CYCLES) + 1.0) / (2.0 * CYCLES)
    bearing = 2.0 * math.pi / ANGLES * np.arange(ANGLES)
    index = np.arange(SHIFTS)
    shift_x = (index // 3 - 1).astype(np.float64)
    shift_y = (index % 3 - 1).astype(np.float64)
    along = shift_x[:, None] * np.cos(bearing) + shift_y[:, None] * np.sin(bearing)
    phase = (-2.0 * math.pi * radius[None, :, None] * along[:, None, :]).reshape(SHIFTS, HALF)
    return np.cos(phase).astype(np.float32), np.sin(phase).astype(np.float32)


def split_numpy(values):
    high = values.astype(jnp.bfloat16)
    rest = values - high.astype(np.float32)
    middle = rest.astype(jnp.bfloat16)
    low = (rest - middle.astype(np.float32)).astype(jnp.bfloat16)
    return high, middle, low


def constant_tables():
    phase_cos, phase_sin = phase_numpy()
    firsts = [first for first, second in PAIRS]
    pair_rows = np.concatenate([phase_cos[firsts], phase_sin[firsts]], axis=0)
    low_lane = np.arange(FOLDED) % ANGLES < BEND
    pair_rows = np.where(low_lane, pair_rows[:, :FOLDED], pair_rows[:, FOLDED:])
    both = np.concatenate([phase_cos, phase_sin], axis=1)
    chosen_rows = np.zeros((LANES, FEAT), jnp.bfloat16)
    for part, piece in enumerate(split_numpy(both)):
        chosen_rows[part * 16 : part * 16 + SHIFTS] = piece
    spread = np.zeros((LANES, HALF), jnp.bfloat16)
    for part in range(3):
        for k in range(CYCLES):
            spread[part * 32 + k, k * ANGLES : (k + 1) * ANGLES] = 1
    turn = np.zeros((LANES, 8 * LANES), jnp.bfloat16)
    lane = np.arange(LANES)
    for r in range(8):
        turn[lane // ANGLES * ANGLES + (lane - r) % ANGLES, r * LANES + lane] = 1
    bend = np.zeros((LANES, 2 * BEND * LANES), jnp.bfloat16)
    for r in range(BEND):
        source = lane // BEND * BEND + (lane - r) % BEND
        bend[source, r * LANES + lane] = 1
        bend[source, (BEND + r) * LANES + lane] = np.where(lane % BEND < r, -1, 1)
    return pair_rows, chosen_rows, spread, turn, bend


def split3(values):
    high = values.astype(BF16)
    rest = values - high.astype(F32)
    middle = rest.astype(BF16)
    low = (rest - middle.astype(F32)).astype(BF16)
    return high, middle, low


def widen(values, spread):
    high, middle, low = split3(values)
    packed = (
        high.astype(F32)
        + pltpu.roll(middle.astype(F32), 32, 1)
        + pltpu.roll(low.astype(F32), 64, 1)
    )
    return jnp.dot(packed.astype(BF16), spread, preferred_element_type=F32)


def turn_left(values, step, lane):
    near = pltpu.roll(values, LANES - step, 1)
    far = pltpu.roll(values, ANGLES - step, 1)
    return jnp.where(lane % ANGLES < ANGLES - step, near, far)


def fold_half(first, second, lane):
    low = lane % ANGLES < BEND
    here = jnp.where(low, first, second)
    there = turn_left(jnp.where(low, second, first), BEND, lane)
    return here + there, here - there


def kernel(blk_size, grp_size, *refs):
    hbm = refs[:14]
    refs_hbm = hbm[11]
    evidence_ref, out_ref = refs[14:16]
    local = refs[16:27]
    (
        images_ref,
        defocus_ref,
        class_ref,
        rotation_ref,
        shift_ref,
        owner_ref,
        noise_ref,
        prior_ref,
        pair_ref,
        table_ref,
        spread_ref,
    ) = local
    (
        turn_ref,
        bend_ref,
        sides,
        held,
        joined,
        base,
        folded,
        shifted,
        picked_rows,
        rotated,
        rotated_low,
        cross_a,
        cross_b,
        unturned,
        stat_send,
        stats,
        part_send,
        parts,
        load_sem,
        ref_ssem,
        ref_rsem,
        stat_ssem,
        stat_rsem,
        part_ssem,
        part_rsem,
    ) = refs[27:]
    my_blk = lax.axis_index("blk")
    my_grp = lax.axis_index("grp")
    rows = images_ref.shape[0]
    own = refs_hbm.shape[0]
    classes = own * blk_size
    half_rows = classes * BEND

    loads = [
        pltpu.make_async_copy(source, place, load_sem.at[number])
        for number, (source, place) in enumerate(
            zip(hbm, local + (held.at[my_blk], turn_ref, bend_ref))
        )
    ]
    for load in loads:
        load.start()

    barrier = pltpu.get_barrier_semaphore()
    for d in range(1, blk_size):
        pl.semaphore_signal(
            barrier, inc=1, device_id={"blk": lax.rem(my_blk + d, blk_size)}, device_id_type=MESH
        )
    for d in range(1, grp_size):
        pl.semaphore_signal(
            barrier, inc=1, device_id={"grp": lax.rem(my_grp + d, grp_size)}, device_id_type=MESH
        )
    pl.semaphore_wait(barrier, blk_size + grp_size - 2)

    def ref_copy(d):
        return pltpu.make_async_remote_copy(
            src_ref=refs_hbm,
            dst_ref=held.at[my_blk],
            send_sem=ref_ssem.at[d],
            recv_sem=ref_rsem.at[d],
            device_id={"blk": lax.rem(my_blk + d, blk_size)},
            device_id_type=MESH,
        )

    for d in range(1, blk_size):
        ref_copy(d).start()

    for load in loads:
        load.wait()
    sides[...] = jnp.zeros(sides.shape, F32)
    sides[0:1, :CYCLES] = noise_ref[...]
    sides[8:9, :CYCLES] = prior_ref[...]
    sides[16:17, :classes] = owner_ref[...].astype(F32)

    rotation = rotation_ref[...]
    local_class = class_ref[...] - my_grp * classes
    member = (local_class >= 0) & (local_class < classes)
    target = jnp.where(member, rotation % BEND * classes + local_class, -1)
    side = jnp.where(rotation < BEND, 1.0, -1.0)
    wide_row = lax.broadcasted_iota(jnp.int32, (LANES, rows), 0)
    slot = jnp.dot(
        sides[16:24, :].astype(BF16),
        jnp.where(wide_row == local_class, 1.0, 0.0).astype(BF16),
        preferred_element_type=F32,
    )[0:1].astype(jnp.int32)
    slot = jnp.where(member, rotation % 8 * classes + slot, -1)

    cycle = lax.broadcasted_iota(jnp.int32, (32, rows), 0)
    frequency = (cycle.astype(F32) + 1.0) / CYCLES
    tall = jnp.where(
        cycle < CYCLES, -jnp.sin(defocus_ref[...] * (frequency * frequency) + 0.15), 0.0
    )
    empty = jnp.zeros((32, rows), F32)
    pieces = [piece.astype(F32) for piece in split3(tall)]
    packed = jnp.concatenate(pieces + [empty], axis=0).T.astype(BF16)
    contrast = jnp.concatenate([tall, empty, empty, empty], axis=0).T
    marks = jnp.where((wide_row % 16 == shift_ref[...]) & (wide_row < 48), 1.0, 0.0)
    marks = jnp.where((wide_row == 48) & (rotation >= 16), 1.0, marks)
    marks = jnp.where((wide_row == 49) & (rotation % 16 >= 8), 1.0, marks).T

    spread = spread_ref[...]
    wide = jnp.dot(packed, spread, preferred_element_type=F32)
    images = images_ref[...].astype(F32)
    base[:, :HALF] = images[:, :HALF] * wide
    base[:, HALF:] = images[:, HALF:] * wide

    lane = lax.broadcasted_iota(jnp.int32, (rows, LANES), 1)
    score_unit = math.log2(math.e) / math.sqrt(FEAT)
    noise_row = sides[0:8, :] * score_unit
    wide_noise = widen(sides[0:8, :], spread)[0:1]

    def weighted(column, part):
        at = column * LANES
        first = part * HALF + at
        scaled = base[:, first : first + LANES] * wide_noise[:, at : at + LANES]
        return scaled.astype(BF16).astype(F32)

    for j in range(FOLDS):
        for part in range(2):
            even, odd = fold_half(weighted(j, part), weighted(j + FOLDS, part), lane)
            place = part * FOLDED + j * LANES
            folded[:, place : place + LANES] = even
            folded[:, HALF + place : HALF + place + LANES] = odd

    def shift_rows(step, carry):
        start = pl.multiple_of(step * 16, 16)
        here = pl.ds(start, 16)
        for column in range(FOLDS):
            begin = column * LANES
            at = [slice(begin + n * FOLDED, begin + n * FOLDED + LANES) for n in range(4)]
            even_re, even_im, odd_re, odd_im = [folded[here, place] for place in at]
            for place, value in zip(at, (even_re, even_im, odd_re, odd_im)):
                shifted[SHIFTS // 2, here, place] = value.astype(BF16)
            for number, (first, second) in enumerate(PAIRS):
                cos_row = pair_ref[number : number + 1, at[0]]
                sin_row = pair_ref[4 + number : 5 + number, at[0]]
                for place, still, moved in (
                    (at[0], even_re, odd_im),
                    (at[1], even_im, -odd_re),
                    (at[2], odd_re, even_im),
                    (at[3], odd_im, -even_re),
                ):
                    left = cos_row * still
                    right = sin_row * moved
                    shifted[first, here, place] = (left + right).astype(BF16)
                    shifted[second, here, place] = (left - right).astype(BF16)
        return carry

    lax.fori_loop(0, rows // 16, shift_rows, 0)

    for d in range(1, blk_size):
        ref_copy(d).wait_recv()
    for b in range(blk_size):
        joined[b * own : (b + 1) * own, :] = held[b]
    whole_refs = joined[...]
    class_lane = lax.broadcasted_iota(jnp.int32, (classes, LANES), 1)
    evens, odds = [], []
    for part in range(2):
        scaled = whole_refs[:, part * HALF : (part + 1) * HALF] * (0.5 * score_unit)
        for j in range(FOLDS):
            even, odd = fold_half(
                scaled[:, j * LANES : (j + 1) * LANES],
                scaled[:, FOLDED + j * LANES : FOLDED + (j + 1) * LANES],
                class_lane,
            )
            evens.append(even)
            odds.append(odd)
    stacks = [jnp.concatenate(pieces, axis=0) for pieces in (evens, odds)]
    highs = [stack.astype(BF16) for stack in stacks]
    lows = [(stack - high.astype(F32)).astype(BF16) for stack, high in zip(stacks, highs)]

    def rotate(sources, place_ref):
        for r in range(0, BEND, 2):
            for part in range(2):
                begin = (part * BEND + r) * LANES
                spun = jnp.dot(
                    sources[part],
                    bend_ref[:, begin : begin + 2 * LANES],
                    preferred_element_type=F32,
                ).astype(BF16)
                for e in range(2):
                    for j in range(2 * FOLDS):
                        place = part * HALF + j * LANES
                        place_ref[
                            (r + e) * classes : (r + e + 1) * classes, place : place + LANES
                        ] = spun[j * classes : (j + 1) * classes, e * LANES : (e + 1) * LANES]

    rotate(highs, rotated)
    square = whole_refs[:, :HALF] * whole_refs[:, :HALF] + whole_refs[:, HALF:] * whole_refs[:, HALF:]
    power = sum(
        lax.dot_general(piece, spread, NT, preferred_element_type=F32) for piece in split3(square)
    )
    penalty = jnp.dot(
        power * (noise_row[0:1] * 0.5),
        jnp.concatenate([tall * tall, empty, empty, empty], axis=0),
        precision=lax.Precision.HIGHEST,
        preferred_element_type=F32,
    )

    def score(t, cross, turned_refs):
        for part in range(2):
            cross[part * half_rows : (part + 1) * half_rows, :] = lax.dot_general(
                turned_refs[:, part * HALF : (part + 1) * HALF],
                shifted[t, :, part * HALF : (part + 1) * HALF],
                NT,
                preferred_element_type=F32,
            )

    def both(cross, r):
        even = cross[r * classes : (r + 1) * classes, :]
        odd = cross[half_rows + r * classes : half_rows + (r + 1) * classes, :]
        return even, odd

    def fold(cross, running):
        peak, total = running
        even, odd = both(cross, 0)
        most = even + jnp.abs(odd)
        for r in range(1, BEND):
            even, odd = both(cross, r)
            most = jnp.maximum(most, even + jnp.abs(odd))
        new_peak = jnp.maximum(peak, jnp.max(most - penalty, axis=0, keepdims=True))
        lowered = penalty + new_peak
        added = jnp.zeros((classes, rows), F32)
        for r in range(BEND):
            even, odd = both(cross, r)
            even = even - lowered
            added = added + (jnp.exp2(even + odd) + jnp.exp2(even - odd))
        total = total * jnp.exp2(peak - new_peak) + jnp.sum(added, axis=0, keepdims=True)
        return new_peak, total

    def visit(step, running):
        score(2 * step + 1, cross_b, rotated)
        running = fold(cross_a, running)
        score(2 * step + 2, cross_a, rotated)
        return fold(cross_b, running)

    score(0, cross_a, rotated)
    running = lax.fori_loop(
        0,
        SHIFTS // 2,
        visit,
        (jnp.full((1, rows), -1e30, F32), jnp.zeros((1, rows), F32)),
    )
    peak, total = fold(cross_a, running)

    stat_send[...] = jnp.concatenate([peak, total, jnp.zeros((6, rows), F32)], axis=0)

    def stat_copy(d):
        return pltpu.make_async_remote_copy(
            src_ref=stat_send,
            dst_ref=stats.at[my_grp],
            send_sem=stat_ssem.at[d],
            recv_sem=stat_rsem.at[d],
            device_id={"grp": lax.rem(my_grp + d, grp_size)},
            device_id_type=MESH,
        )

    for d in range(1, grp_size):
        stat_copy(d).start()
    stats[my_grp] = stat_send[...]

    turns = jnp.dot(marks.astype(BF16), table_ref[...], preferred_element_type=F32)
    far_turn = jnp.broadcast_to(marks[:, 48:49], (rows, LANES)) > 0.5
    near_turn = jnp.broadcast_to(marks[:, 49:50], (rows, LANES)) > 0.5

    def keep(part, first):
        high = part.astype(BF16)
        low = (part - high.astype(F32)).astype(BF16)
        picked_rows[:rows, first : first + LANES] = high
        picked_rows[rows : 2 * rows, first : first + LANES] = low
        picked_rows[2 * rows :, first : first + LANES] = high

    keep(contrast * contrast, FEAT)
    for j in range(FOLDS):
        moved = []
        for column in (j, j + FOLDS):
            at_re = slice(column * LANES, (column + 1) * LANES)
            at_im = slice(HALF + column * LANES, HALF + (column + 1) * LANES)
            real = base[:, at_re]
            imag = base[:, at_im]
            for part, at in (
                (turns[:, at_re] * real + turns[:, at_im] * imag, at_re),
                (turns[:, at_re] * imag - turns[:, at_im] * real, at_im),
            ):
                part = jnp.where(far_turn, turn_left(part, 16, lane), part)
                part = jnp.where(near_turn, turn_left(part, 8, lane), part)
                keep(part, at.start)
            real = weighted(column, 0)
            imag = weighted(column, 1)
            moved.append(turns[:, at_re] * real + turns[:, at_im] * imag)
            moved.append(turns[:, at_re] * imag - turns[:, at_im] * real)
        for part in range(2):
            place = part * FOLDED + j * LANES
            for number, value in enumerate(fold_half(moved[part], moved[part + 2], lane)):
                first = number * HALF + place
                high = value.astype(BF16)
                shifted[SHIFTS, :, first : first + LANES] = high
                shifted[SHIFTS + 1, :, first : first + LANES] = (
                    value - high.astype(F32)
                ).astype(BF16)
    rotate(lows, rotated_low)
    score(SHIFTS, cross_b, rotated)
    score(SHIFTS, cross_a, rotated_low)
    class_row = lax.broadcasted_iota(jnp.int32, (classes, rows), 0)

    def pick(cross, chosen_sum, offset):
        for r in range(BEND):
            even, odd = both(cross, r)
            chosen_sum = chosen_sum + jnp.where(
                class_row + r * classes == target, even + side * odd - offset, 0.0
            )
        return chosen_sum

    chosen_sum = pick(cross_b, jnp.zeros((classes, rows), F32), penalty)
    score(SHIFTS + 1, cross_b, rotated)
    chosen_sum = pick(cross_a, chosen_sum, 0.0)
    chosen_sum = pick(cross_b, chosen_sum, 0.0)
    picked = jnp.sum(chosen_sum, axis=0, keepdims=True)

    for d in range(1, grp_size):
        stat_copy(d).wait_recv()
    peaks = [stats[g][0:1] for g in range(grp_size)]
    totals = [stats[g][1:2] for g in range(grp_size)]
    top = functools.reduce(jnp.maximum, peaks)
    whole = sum(t * jnp.exp2(p - top) for p, t in zip(peaks, totals))
    log_sum = top + jnp.log2(whole)
    orients = classes * grp_size * ANGLES * SHIFTS
    evidence_ref[...] = log_sum * math.log(2.0) - math.log(orients)
    weight = jnp.where(target >= 0, jnp.exp2(jnp.minimum(picked - log_sum, 16.0)) * orients, 0.0)

    turned_row = lax.broadcasted_iota(jnp.int32, (8 * classes, rows), 0)
    placed = jnp.where(turned_row == slot, weight, 0.0)
    placed_high = placed.astype(BF16)
    placed_low = (placed - placed_high.astype(F32)).astype(BF16)
    left = jnp.concatenate([placed_high, placed_high, placed_low], axis=1)
    count = CHUNKS * classes
    for j in range(0, CHUNKS, 2):
        block = jnp.dot(
            left, picked_rows[:, j * LANES : (j + 2) * LANES], preferred_element_type=F32
        )
        high = block.astype(BF16)
        low = (block - high.astype(F32)).astype(BF16)
        for e in range(2):
            first = (j + e) * classes
            for r in range(8):
                at = (slice(r * classes, (r + 1) * classes), slice(e * LANES, (e + 1) * LANES))
                unturned[first : first + classes, r * LANES : (r + 1) * LANES] = high[at]
                unturned[count + first : count + first + classes, r * LANES : (r + 1) * LANES] = (
                    low[at]
                )
    block = jnp.dot(left, picked_rows[:, FEAT:], preferred_element_type=F32)
    denominator = block[0:classes]
    for r in range(1, 8):
        denominator = denominator + block[r * classes : (r + 1) * classes]
    sums = lax.dot_general(unturned[...], turn_ref[...], NT, preferred_element_type=F32)
    sums = sums[:count] + sums[count:]
    for b in range(blk_size):
        for j in range(CHUNKS):
            part_send[b, :, j * LANES : (j + 1) * LANES] = sums[
                j * classes + b * own : j * classes + (b + 1) * own
            ]
        part_send[b, :, FEAT:] = denominator[b * own : (b + 1) * own]

    def part_copy(d):
        peer = lax.rem(my_blk + d, blk_size)
        return pltpu.make_async_remote_copy(
            src_ref=part_send.at[peer],
            dst_ref=parts.at[d],
            send_sem=part_ssem.at[d],
            recv_sem=part_rsem.at[d],
            device_id={"blk": peer},
            device_id_type=MESH,
        )

    for d in range(1, blk_size):
        part_copy(d).start()
    gathered = part_send[my_blk]
    for d in range(1, blk_size):
        part_copy(d).wait_recv()
        gathered = gathered + parts[d]
    lower = gathered[:, FEAT:] + sides[8:9, :]
    lower = jnp.concatenate([lower, jnp.ones((8 - own, LANES), F32)], axis=0)
    lane8 = lax.broadcasted_iota(jnp.int32, (8, LANES), 1)
    lower = widen(jnp.where(lane8 < CYCLES, lower, 0.0), spread)[:own]
    out_ref[:, :HALF] = gathered[:, :HALF] / lower
    out_ref[:, HALF:] = gathered[:, HALF:FEAT] / lower
    for d in range(1, blk_size):
        ref_copy(d).wait_send()
        part_copy(d).wait_send()
    for d in range(1, grp_size):
        stat_copy(d).wait_send()


def pass_on(first_in, second_in, first_out, second_out, sem):
    copies = [
        pltpu.make_async_copy(first_in, first_out, sem.at[0]),
        pltpu.make_async_copy(second_in, second_out, sem.at[1]),
    ]
    for copy in copies:
        copy.start()
    for copy in copies:
        copy.wait()


def shards(images, defocus, class_id, rotation_id, shift_id, references, owner, inv_noise, prior):
    rows = images.shape[0]
    own = references.shape[1]
    blk_size = lax.axis_size("blk")
    grp_size = lax.axis_size("grp")
    classes = owner.shape[1]
    turned = classes * ANGLES
    operands = [
        images,
        defocus.reshape(1, rows),
        class_id.reshape(1, rows),
        rotation_id.reshape(1, rows),
        shift_id.reshape(1, rows),
        owner,
        inv_noise.reshape(1, CYCLES),
        prior.reshape(1, CYCLES),
        *[jnp.asarray(table) for table in constant_tables()[:3]],
        references[0],
        *[jnp.asarray(table) for table in constant_tables()[3:]],
    ]
    vmem = pl.BlockSpec(memory_space=pltpu.VMEM)
    whole = pl.BlockSpec(memory_space=pl.ANY)
    outs = (
        jax.ShapeDtypeStruct((1, rows), F32),
        jax.ShapeDtypeStruct((own, FEAT), F32),
    )
    evidence, new_refs = pl.pallas_call(
        functools.partial(kernel, blk_size, grp_size),
        out_shape=outs,
        in_specs=[whole] * 14,
        out_specs=(vmem, vmem),
        scratch_shapes=[
            *[pltpu.VMEM(operand.shape, operand.dtype) for operand in operands[:11]],
            pltpu.VMEM(operands[12].shape, BF16),
            pltpu.VMEM(operands[13].shape, BF16),
            pltpu.VMEM((24, LANES), F32),
            pltpu.VMEM((blk_size, own, FEAT), F32),
            pltpu.VMEM((classes, FEAT), F32),
            pltpu.VMEM((rows, FEAT), F32),
            pltpu.VMEM((rows, FEAT), F32),
            pltpu.VMEM((SHIFTS + 2, rows, FEAT), BF16),
            pltpu.VMEM((3 * rows, FEAT + LANES), BF16),
            pltpu.VMEM((turned // 2, FEAT), BF16),
            pltpu.VMEM((turned // 2, FEAT), BF16),
            pltpu.VMEM((turned, rows), F32),
            pltpu.VMEM((turned, rows), F32),
            pltpu.VMEM((2 * CHUNKS * classes, 8 * LANES), BF16),
            pltpu.VMEM((8, rows), F32),
            pltpu.VMEM((grp_size, 8, rows), F32),
            pltpu.VMEM((blk_size, own, FEAT + LANES), F32),
            pltpu.VMEM((blk_size, own, FEAT + LANES), F32),
            pltpu.SemaphoreType.DMA((14,)),
            pltpu.SemaphoreType.DMA((blk_size,)),
            pltpu.SemaphoreType.DMA((blk_size,)),
            pltpu.SemaphoreType.DMA((grp_size,)),
            pltpu.SemaphoreType.DMA((grp_size,)),
            pltpu.SemaphoreType.DMA((blk_size,)),
            pltpu.SemaphoreType.DMA((blk_size,)),
        ],
        compiler_params=pltpu.CompilerParams(
            collective_id=0, has_side_effects=True, vmem_limit_bytes=60 * 1024 * 1024
        ),
    )(*operands)
    evidence, new_refs = pl.pallas_call(
        pass_on,
        out_shape=outs,
        in_specs=[whole] * 2,
        out_specs=(whole, whole),
        scratch_shapes=[pltpu.SemaphoreType.DMA((2,))],
    )(evidence, new_refs)
    return (evidence[0], new_refs[None])


def solution(mesh):
    in_specs = (
        P("blk", None),
        P("blk"),
        P("blk", None),
        P("blk"),
        P("blk"),
        P("grp", "blk", None),
        P("grp", None),
        P(),
        P(),
    )
    out_specs = (P("blk"), P("grp", "blk", None))
    return jax.shard_map(shards, mesh=mesh, in_specs=in_specs, out_specs=out_specs, check_vma=False)
```

time: 330 us -> 26.8 us (0.08)
  local copies, waits for them, and re-layouts: 94.8 us -> 0 us
  other arithmetic: 70.8 us -> 0 us
  blocking collectives: 66.4 us -> 0 us
  waiting for transfers between devices: 46.5 us -> 0 us
  matrix products: 33.3 us -> 0 us
  Pallas kernels: 0 us -> 26 us
  between operations: 15 us -> 0.64 us
    convert_element_type x8 -> x0, local copies, waits for them, and re-layouts: 71.3 us -> none  [make_templates(): stacked.reshape(block_rows * ANGLES * SHIFTS, -1).astype(jnp.bfloat16)]
    another operation x17 -> x0, other arithmetic: 51.4 us -> none  [the longest x8 34.9 us: make_templates(): stacked = jnp.stack([real_part, imag_part], axis=3)]
    unnamed x2 -> x0, waiting for transfers between devices: 46.5 us -> none
    dot_general x29 -> x0, matrix products: 33.3 us -> none  [the longest x8 14.4 us: score_block(): lax.dot_general(templates, weighted, (((1,), (1,)), ((), ())), preferred_...]
    all_gather x1 -> x0, blocking collectives: 32.3 us -> none  [shards(): shard_piece = lax.all_gather(references, 'blk', axis=1, tiled=True)]
    pallas_call x0 -> x2, Pallas kernels: none -> 26 us  [the longest x1 24.5 us: shards(): pl.pallas_call(functools.partial(kernel, blk_size, grp_size), out_shape=o...]
    unnamed x1 -> x0, blocking collectives: 21.7 us -> none
    psum x1 -> x0, blocking collectives: 6.78 us -> none  [shards(): global_total = lax.psum(total * jnp.exp(peak - global_peak), 'grp')]
  transfers between devices with their start and end apart: 1 -> 0, of which waited for: 1 -> 0; matrix products, arithmetic and copies ran while one was open for 0% -> 0% of each run, Pallas kernels for 0% -> 0%
where the time goes in v1:
time: 26.8 us; the launch traced here: 26.7 us
  Pallas kernels  26 us (97%)
  between operations  0.64 us (2%)
    pallas_call x1, Pallas kernels, shards(): pl.pallas_call(functools.partial(kernel, blk_size, grp_size), out_shape=o...  24.5 us
    pallas_call x1, Pallas kernels, shards(): pl.pallas_call(pass_on, out_shape=outs, in_specs=[whole] * 2, out_specs=(...  1.52 us

profile of v1, /device:TPU:0, one launch (start us, length us, event | category | flops | bytes accessed | tf_op | source)
XLA Modules:
  0.0 26.7 jit_solution(17019784902700010090)
XLA Ops:
  0.6 24.5 %shard_map.149 = (f32[1,256]{1,0:T(1,128)}, f32[2,1536]{1,0:T(2,128)}) custom-call(bf16[256,1536]{1,0:T(8,128)(2,1)} %refs_0_.1, f32[1,256]{1,0:T(1,128)} %bitcast.10, s32[1,256]{1,0:T(1,128)} %bitcast.11, s32[1,256]{1,0:T(1,128)} %bitcast.12, s32[1,256]{1,0:T(1,128)} %bitcast.13, s32[1,16]{1,0:T(1,128)} %refs_5_.1, f32[1,24]{1,0:T(1,128)} %bitcast.14, ...), custom_call_target="tpu_custom_call" | custom-call | tf_op jit(solution)/shard_map/pallas_call | solution.py:553
  25.2 1.5 %shard_map.150 = (f32[1,256]{1,0:T(1,128)}, f32[2,1536]{1,0:T(2,128)}) custom-call(f32[1,256]{1,0:T(1,128)} %get-tuple-element.6.first_in, f32[2,1536]{1,0:T(2,128)} %get-tuple-element.7.second_in), custom_call_target="tpu_custom_call" | custom-call | tf_op jit(solution)/shard_map/pallas_call | solution.py:590
